TPU v7x, 32 devices: a whole 2x2x4 slice. The times are simulated.
32 devices in a mesh: slide: 2 (over x), row: 8 (over z, y), col: 2 (over core).
Axes of the slice: x: 2, y: 2, z: 4, core: 2. Of those that a mesh axis runs over, the one named last changes fastest.
Arguments:
- features: bfloat16 [32768, 1024], P(('slide', 'row', 'col')), parts along dimension 0, may hold values from -6 to 6
- seq_order: int32 [32, 1024], P(('slide', 'row', 'col')), parts along dimension 0, may hold values from 0 to 1023, each once within a row
- block_links: int32 [9, 32, 8], P(None, ('slide', 'row'), 'col'), parts along dimension 1, may hold values 0 or 1
- start_vectors: float32 [32, 32, 1024], P(None, ('slide', 'row'), 'col'), parts along dimension 1, may hold values from -6 to 6
Outputs:
- eigen_fields: float32 [32, 32, 1024], P(None, ('slide', 'row'), 'col'), parts along dimension 1
There are 2 independent parts, one for each index of `slide`. A program takes and returns all parts, laid end to end along the dimension named above; each array names one. Nothing has to cross between parts.
Inputs may be any that keep to these rules, and one draw needn't show every extreme that they name: Each row of seq_order lists every number of 0 to 1023 once. `block_links`: entries of the centre offset 4 are not read.
All inputs are finite; a program needn't handle non-finite values. No bound on the sum of `block_links` on one device may be relied on, other than what follows from the above.
Results may differ from a plain program's by a relative error of at most 0.0021.
Values may be sent and summed in bfloat16 or wider, within the bound.
A program may use at most 64 MiB of HBM per device.

v0:
```python
import math

import jax
import jax.numpy as jnp
from jax import lax
from jax.sharding import PartitionSpec as P

ITERS = 3


SHARPNESS = 4.0
EPSILON = 1e-06


def padded_2(x, sides, width):
    for axis, dim in sides:
        peers, length = (lax.axis_size(axis), x.shape[dim])
        up = [(i, (i + 1) % peers) for i in range(peers - 1)]
        down = [(j, i) for i, j in up]
        last = lax.slice_in_dim(x, length - width, length, axis=dim)
        leading = lax.slice_in_dim(x, 0, width, axis=dim)
        before = lax.ppermute(last, axis, up)
        after = lax.ppermute(leading, axis, down)
        x = jnp.concatenate([before, x, after], axis=dim)
    return x


def body(features, seq_order, block_links, start_vectors):
    rows_n = lax.axis_size("row")
    cols_n = lax.axis_size("col")
    feat_w = features.shape[1]
    vec_n, tile_h, tile_w = start_vectors.shape
    blocks_n = block_links.shape[2]
    block_w = tile_w // blocks_n
    height = tile_h * rows_n
    strip_w = tile_w // rows_n
    wide = features.astype(jnp.float32)
    squares = jnp.sum(wide * wide, axis=1, keepdims=True)
    unit_rows = (wide * lax.rsqrt(squares + EPSILON)).astype(jnp.bfloat16)
    placed = jnp.take(unit_rows, seq_order[0], axis=0).reshape(height, strip_w, feat_w)
    arrived = lax.all_to_all(placed, "row", split_axis=0, concat_axis=1, tiled=True)
    arrived = arrived.reshape(tile_h, blocks_n, block_w, feat_w)
    padded = padded_2(arrived, (("row", 0), ("col", 1)), 1)
    center = padded[1 : tile_h + 1, 1 : blocks_n + 1]
    row_pos = lax.axis_index("row") * tile_h + jnp.arange(tile_h)
    col_pos = lax.axis_index("col") * blocks_n + jnp.arange(blocks_n)
    tile_list = []
    for offset in range(9):
        step_row = offset // 3 - 1
        step_col = offset % 3 - 1
        shifted = padded[
            1 + step_row : 1 + step_row + tile_h, 1 + step_col : 1 + step_col + blocks_n
        ]
        dots = jnp.einsum("abid,abjd->abij", center, shifted, preferred_element_type=jnp.float32)
        inside = ((row_pos + step_row >= 0) & (row_pos + step_row < height))[:, None] & (
            (col_pos + step_col >= 0) & (col_pos + step_col < blocks_n * cols_n)
        )[None, :]
        chosen = inside if offset == 4 else inside & (block_links[offset] == 1)
        tile_list.append(
            jnp.exp(SHARPNESS * (dots - 1.0)) * chosen.astype(jnp.float32)[:, :, None, None]
        )
    tiles = jnp.stack(tile_list)
    degree = jnp.sum(tiles, axis=(0, 4))

    def propagate(field):
        rimmed = padded_2(field, (("row", 1), ("col", 2)), 1)
        total = jnp.zeros_like(field)
        for offset in range(9):
            step_row = offset // 3 - 1
            step_col = offset % 3 - 1
            shifted = rimmed[
                :, 1 + step_row : 1 + step_row + tile_h, 1 + step_col : 1 + step_col + blocks_n
            ]
            total = total + jnp.einsum(
                "abij,kabj->kabi", tiles[offset], shifted, precision=lax.Precision.HIGHEST
            )
        return total / degree

    def solve_lower(lower_factor, field):
        flat = field.reshape(vec_n, -1)
        return jax.scipy.linalg.solve_triangular(lower_factor, flat, lower=True).reshape(
            field.shape
        )

    vectors = start_vectors.reshape(vec_n, tile_h, blocks_n, block_w)
    grown = propagate(vectors)
    for step in range(ITERS):
        factor_flat = grown.reshape(vec_n, -1)
        partial_gram = jnp.dot(factor_flat, factor_flat.T, precision=lax.Precision.HIGHEST)
        lower_factor = jnp.linalg.cholesky(lax.psum(partial_gram, ("row", "col")))
        if step + 1 < ITERS:
            grown = solve_lower(lower_factor, propagate(grown))
        else:
            vectors = solve_lower(lower_factor, grown)
    scale = math.sqrt(height * tile_w * cols_n)
    return vectors.reshape(vec_n, tile_h, tile_w) * scale


def solution(mesh):
    return jax.shard_map(
        body,
        mesh=mesh,
        in_specs=(
            P(("slide", "row", "col"), None),
            P(("slide", "row", "col"), None),
            P(None, ("slide", "row"), "col"),
            P(None, ("slide", "row"), "col"),
        ),
        out_specs=P(None, ("slide", "row"), "col"),
        check_vma=False,
    )
```

profile of v0, /device:TPU:0, one launch (start us, length us, event | category | flops | bytes accessed | tf_op | source)
XLA Modules:
  0.0 367.6 jit_solution(12635351489948123816)
XLA Ops:
  0.0 2.2 fusion
  4.2 5.4 %gather_fusion = bf16[1024,1024]{1,0:T(8,128)(2,1)} fusion(bf16[1024,1024]{1,0:T(8,128)(2,1)S(1)} %fusion.1, s32[1024]{0:T(1024)S(1)} %broadcast_clamp_fusion), kind=kCustom, calls=%fused_computation | custom fusion | bytes 4198400 | tf_op jit(solution)/shard_map/jit(_take)/gather | solution.py:40
  9.6 3.2 broadcast_select_fusion
  12.7 7.4 %all-to-all-start = ((bf16[16,64,1024]{2,1,0:T(8,128)(2,1)}), bf16[16,64,1024]{2,1,0:T(8,128)(2,1)S(1)}, u32[]{:S(2)}, u32[]{:S(2)}) async-start(bf16[16,64,1024]{2,1,0:T(8,128)(2,1)} %broadcast_select_fusion), calls=%async_computation | async-start | bytes 4194304 | tf_op jit(solution)/shard_map/all_to_all | solution.py:41
  20.3 3.9 %collective-permute-start = (f32[32,1,4,128]{3,0,2,1:T(8,128)S(1)}, f32[32,1,4,128]{3,0,2,1:T(8,128)S(1)}, u32[]{:S(2)}, u32[]{:S(2)}) collective-permute-start(f32[32,1,4,128]{3,0,2,1:T(8,128)S(1)} %get-tuple-element.32), channel_id=1, source_target_pairs={{0,2},{2,4},{4,6},{6,8},{8,10},{10,12},{12,14},{1,3},{3,5},{5,7},{... | collective-permute-start | bytes 196616 | tf_op jit(solution)/shard_map/ppermute | solution.py:22
  24.3 1.3 collective-permute-start.1
  26.2 13.9 %collective-permute-done = f32[32,1,4,128]{3,0,2,1:T(8,128)S(1)} collective-permute-done((f32[32,1,4,128]{3,0,2,1:T(8,128)S(1)}, f32[32,1,4,128]{3,0,2,1:T(8,128)S(1)}, u32[]{:S(2)}, u32[]{:S(2)}) %collective-permute-start) | collective-permute-done | bytes 65568 | tf_op jit(solution)/shard_map/ppermute | solution.py:22
  40.0 29.0 %all-to-all-done = bf16[16,64,1024]{2,1,0:T(8,128)(2,1)S(1)} async-done(((bf16[16,64,1024]{2,1,0:T(8,128)(2,1)}), bf16[16,64,1024]{2,1,0:T(8,128)(2,1)S(1)}, u32[]{:S(2)}, u32[]{:S(2)}) %all-to-all-start) | async-done | bytes 2097184 | tf_op jit(solution)/shard_map/all_to_all | solution.py:41
  69.2 2.7 collective-permute-start.3
  72.0 1.3 collective-permute-start.4
  73.4 1.3 collective-permute-start.6
  74.7 3.0 collective-permute-start.2
  79.2 36.8 %collective-permute-done.3 = bf16[1,4,128,1024]{3,2,1,0:T(8,128)(2,1)S(1)} collective-permute-done((bf16[1,4,128,1024]{3,2,1,0:T(8,128)(2,1)S(1)}, bf16[1,4,128,1024]{3,2,1,0:T(8,128)(2,1)S(1)}, u32[]{:S(2)}, u32[]{:S(2)}) %collective-permute-start.3) | collective-permute-done | bytes 1048608 | tf_op jit(solution)/shard_map/ppermute | solution.py:22
  116.3 1.4 collective-permute-start.5
  117.6 1.5 collective-permute-start.7
  122.2 1.4 maximum_maximum_fusion
  133.7 62.7 %psum.21 = f32[32,32]{0,1:T(8,128)S(1)} all-reduce(f32[32,32]{0,1:T(8,128)S(1)} %convolution_bitcast_fusion.5), channel_id=1, replica_groups=mesh['slide'=2,'row'=8,'col'=2] {'row','col'}, use_global_device_ids=true, to_apply=%region_10.11 | all-reduce | flops 1024 | bytes 8192 | tf_op jit(solution)/shard_map/psum | solution.py:90
  196.4 2.9 cholesky.59
  201.3 1.3 collective-permute-start.9
  203.1 3.1 custom-call.7
  207.5 1.3 collective-permute-start.11
  208.8 3.3 collective-permute-start.10
  219.4 57.7 %psum.22 = f32[32,32]{0,1:T(8,128)S(1)} all-reduce(f32[32,32]{0,1:T(8,128)S(1)} %fusion.227), channel_id=1, replica_groups=mesh['slide'=2,'row'=8,'col'=2] {'row','col'}, use_global_device_ids=true, to_apply=%region_13.16 | all-reduce | flops 1024 | bytes 8192 | tf_op jit(solution)/shard_map/psum | solution.py:90
  277.2 2.9 cholesky.70
  283.4 2.4 custom-call.8
  285.9 1.4 collective-permute-start.13
  287.4 5.0 %collective-permute-done.13 = f32[32,1,4,128]{3,0,2,1:T(8,128)S(1)} collective-permute-done((f32[32,1,4,128]{3,0,2,1:T(8,128)}, f32[32,1,4,128]{3,0,2,1:T(8,128)S(1)}, u32[]{:S(2)}, u32[]{:S(2)}) %collective-permute-start.13) | collective-permute-done | bytes 65568 | tf_op jit(solution)/shard_map/ppermute | solution.py:23
  292.4 1.3 collective-permute-start.15
  293.7 3.0 collective-permute-start.14
  302.1 57.6 %psum.23 = f32[32,32]{0,1:T(8,128)S(1)} all-reduce(f32[32,32]{0,1:T(8,128)S(1)} %fusion.228), channel_id=1, replica_groups=mesh['slide'=2,'row'=8,'col'=2] {'row','col'}, use_global_device_ids=true, to_apply=%region_14.17 | all-reduce | flops 1024 | bytes 8192 | tf_op jit(solution)/shard_map/psum | solution.py:90
  359.8 2.9 cholesky.81
  364.0 2.4 custom-call.9
  (141 shorter events, 40.0 us)
Async XLA Ops:
  0.0 2.2 copy-start
  2.2 0.7 copy-start.14
  12.7 7.4 %copy-start.13 = (f32[32,2,512]{2,1,0:T(2,128)S(1)}, f32[32,2,512]{2,1,0:T(2,128)}, u32[]{:S(2)}) copy-start(f32[32,2,512]{2,1,0:T(2,128)} %param.10) | copy-start | bytes 393220
  12.7 12.9 %copy-start.12 = (s32[9,2,4]{0,2,1:T(4,128)S(1)}, s32[9,2,4]{0,2,1:T(4,128)}, u32[]{:S(2)}) copy-start(s32[9,2,4]{0,2,1:T(4,128)} %param.9) | copy-start | bytes 868
  12.7 56.4 %all-to-all-start = ((bf16[16,64,1024]{2,1,0:T(8,128)(2,1)}), bf16[16,64,1024]{2,1,0:T(8,128)(2,1)S(1)}, u32[]{:S(2)}, u32[]{:S(2)}) async-start(bf16[16,64,1024]{2,1,0:T(8,128)(2,1)} %broadcast_select_fusion), calls=%async_computation | async-start | bytes 4194304 | tf_op jit(solution)/shard_map/all_to_all | solution.py:41
  20.3 19.7 %collective-permute-start = (f32[32,1,4,128]{3,0,2,1:T(8,128)S(1)}, f32[32,1,4,128]{3,0,2,1:T(8,128)S(1)}, u32[]{:S(2)}, u32[]{:S(2)}) collective-permute-start(f32[32,1,4,128]{3,0,2,1:T(8,128)S(1)} %get-tuple-element.32), channel_id=1, source_target_pairs={{0,2},{2,4},{4,6},{6,8},{8,10},{10,12},{12,14},{1,3},{3,5},{5,7},{... | collective-permute-start | bytes 196616 | tf_op jit(solution)/shard_map/ppermute | solution.py:22
  24.3 49.1 %collective-permute-start.1 = (f32[32,1,4,128]{3,0,2,1:T(8,128)S(1)}, f32[32,1,4,128]{3,0,2,1:T(8,128)S(1)}, u32[]{:S(2)}, u32[]{:S(2)}) collective-permute-start(f32[32,1,4,128]{3,0,2,1:T(8,128)S(1)} %get-tuple-element.31), channel_id=1, source_target_pairs={{2,0},{4,2},{6,4},{8,6},{10,8},{12,10},{14,12},{3,1},{5,3},{7,5},{... | collective-permute-start | bytes 196616 | tf_op jit(solution)/shard_map/ppermute | solution.py:23
  69.2 46.8 %collective-permute-start.3 = (bf16[1,4,128,1024]{3,2,1,0:T(8,128)(2,1)S(1)}, bf16[1,4,128,1024]{3,2,1,0:T(8,128)(2,1)S(1)}, u32[]{:S(2)}, u32[]{:S(2)}) collective-permute-start(bf16[1,4,128,1024]{3,2,1,0:T(8,128)(2,1)S(1)} %bitcast.139), channel_id=1, source_target_pairs={{0,2},{2,4},{4,6},{6,8},{8,10},{10,12},{12,14},{1,3},{3,5},{5,7},{... | collective-permute-start | bytes 3145736 | tf_op jit(solution)/shard_map/ppermute | solution.py:22
  72.0 44.0 %collective-permute-start.4 = (bf16[1,4,128,1024]{3,2,1,0:T(8,128)(2,1)S(1)}, bf16[1,4,128,1024]{3,2,1,0:T(8,128)(2,1)S(1)}, u32[]{:S(2)}, u32[]{:S(2)}) collective-permute-start(bf16[1,4,128,1024]{3,2,1,0:T(8,128)(2,1)S(1)} %bitcast.138), channel_id=1, source_target_pairs={{2,0},{4,2},{6,4},{8,6},{10,8},{12,10},{14,12},{3,1},{5,3},{7,5},{... | collective-permute-start | bytes 3145736 | tf_op jit(solution)/shard_map/ppermute | solution.py:23
  73.4 55.9 %collective-permute-start.6 = (f32[32,4,1,128]{3,0,2,1:T(8,128)S(1)}, f32[32,4,1,128]{3,0,2,1:T(8,128)S(1)}, u32[]{:S(2)}, u32[]{:S(2)}) collective-permute-start(f32[32,4,1,128]{3,0,2,1:T(8,128)S(1)} %get-tuple-element.26), channel_id=1, source_target_pairs={{1,0},{3,2},{5,4},{7,6},{9,8},{11,10},{13,12},{15,14},{17,16},{19,... | collective-permute-start | bytes 196616 | tf_op jit(solution)/shard_map/ppermute | solution.py:23
  74.7 53.4 %collective-permute-start.2 = (f32[32,4,1,128]{3,0,2,1:T(8,128)S(1)}, f32[32,4,1,128]{3,0,2,1:T(8,128)S(1)}, u32[]{:S(2)}, u32[]{:S(2)}) collective-permute-start(f32[32,4,1,128]{3,0,2,1:T(8,128)S(1)} %get-tuple-element.25), channel_id=1, source_target_pairs={{0,1},{2,3},{4,5},{6,7},{8,9},{10,11},{12,13},{14,15},{16,17},{18,... | collective-permute-start | bytes 196616 | tf_op jit(solution)/shard_map/ppermute | solution.py:22
  116.3 5.5 %collective-permute-start.5 = (bf16[4,1,128,1024]{3,2,1,0:T(8,128)(2,1)S(1)}, bf16[4,1,128,1024]{3,2,1,0:T(8,128)(2,1)S(1)}, u32[]{:S(2)}, u32[]{:S(2)}) collective-permute-start(bf16[4,1,128,1024]{3,2,1,0:T(8,128)(2,1)S(1)} %get-tuple-element.17), channel_id=1, source_target_pairs={{0,1},{2,3},{4,5},{6,7},{8,9},{10,11},{12,13},{14,15},{16,17},{18,... | collective-permute-start | bytes 3145736 | tf_op jit(solution)/shard_map/ppermute | solution.py:22
  117.6 4.6 %collective-permute-start.7 = (bf16[4,1,128,1024]{3,2,1,0:T(8,128)(2,1)S(1)}, bf16[4,1,128,1024]{3,2,1,0:T(8,128)(2,1)S(1)}, u32[]{:S(2)}, u32[]{:S(2)}) collective-permute-start(bf16[4,1,128,1024]{3,2,1,0:T(8,128)(2,1)S(1)} %get-tuple-element.18), channel_id=1, source_target_pairs={{1,0},{3,2},{5,4},{7,6},{9,8},{11,10},{13,12},{15,14},{17,16},{19,... | collective-permute-start | bytes 3145736 | tf_op jit(solution)/shard_map/ppermute | solution.py:23
  126.6 1.5 copy-start.1
  127.3 1.4 copy-start.7
  128.0 2.9 copy-start.4
  200.0 6.2 %collective-permute-start.8 = (f32[32,1,4,128]{3,0,2,1:T(8,128)}, f32[32,1,4,128]{3,0,2,1:T(8,128)S(1)}, u32[]{:S(2)}, u32[]{:S(2)}) collective-permute-start(f32[32,1,4,128]{3,0,2,1:T(8,128)} %get-tuple-element.29), channel_id=1, source_target_pairs={{0,2},{2,4},{4,6},{6,8},{8,10},{10,12},{12,14},{1,3},{3,5},{5,7},{... | collective-permute-start | bytes 196616 | tf_op jit(solution)/shard_map/ppermute | solution.py:22
  201.3 6.2 %collective-permute-start.9 = (f32[32,1,4,128]{3,0,2,1:T(8,128)S(1)}, f32[32,1,4,128]{3,0,2,1:T(8,128)S(1)}, u32[]{:S(2)}, u32[]{:S(2)}) collective-permute-start(f32[32,1,4,128]{3,0,2,1:T(8,128)S(1)} %get-tuple-element.30), channel_id=1, source_target_pairs={{2,0},{4,2},{6,4},{8,6},{10,8},{12,10},{14,12},{3,1},{5,3},{7,5},{... | collective-permute-start | bytes 196616 | tf_op jit(solution)/shard_map/ppermute | solution.py:23
  206.2 7.0 %copy-start.2 = (f32[2,4,128,128]{2,3,1,0:T(8,128)S(1)}, f32[2,4,128,128]{2,3,1,0:T(8,128)}, u32[]{:S(2)}) copy-start(f32[2,4,128,128]{2,3,1,0:T(8,128)} %copy-done.1) | copy-start | bytes 1572868
  206.2 7.5 %copy-start.8 = (f32[2,4,128,128]{2,3,1,0:T(8,128)S(1)}, f32[2,4,128,128]{2,3,1,0:T(8,128)}, u32[]{:S(2)}) copy-start(f32[2,4,128,128]{2,3,1,0:T(8,128)} %copy-done.7) | copy-start | bytes 1572868
  207.5 6.9 %collective-permute-start.11 = (f32[32,4,1,128]{3,0,2,1:T(8,128)S(1)}, f32[32,4,1,128]{3,0,2,1:T(8,128)S(1)}, u32[]{:S(2)}, u32[]{:S(2)}) collective-permute-start(f32[32,4,1,128]{3,0,2,1:T(8,128)S(1)} %get-tuple-element.24), channel_id=1, source_target_pairs={{1,0},{3,2},{5,4},{7,6},{9,8},{11,10},{13,12},{15,14},{17,16},{19,... | collective-permute-start | bytes 196616 | tf_op jit(solution)/shard_map/ppermute | solution.py:23
  208.8 4.4 %collective-permute-start.10 = (f32[32,4,1,128]{3,0,2,1:T(8,128)S(1)}, f32[32,4,1,128]{3,0,2,1:T(8,128)S(1)}, u32[]{:S(2)}, u32[]{:S(2)}) collective-permute-start(f32[32,4,1,128]{3,0,2,1:T(8,128)S(1)} %get-tuple-element.23), channel_id=1, source_target_pairs={{0,1},{2,3},{4,5},{6,7},{8,9},{10,11},{12,13},{14,15},{16,17},{18,... | collective-permute-start | bytes 196616 | tf_op jit(solution)/shard_map/ppermute | solution.py:22
  212.6 2.3 copy-start.5
  213.1 2.3 copy-start.11
  219.4 78.5 %copy-start.3 = (f32[2,4,128,128]{2,3,1,0:T(8,128)S(1)}, f32[2,4,128,128]{2,3,1,0:T(8,128)}, u32[]{:S(2)}) copy-start(f32[2,4,128,128]{2,3,1,0:T(8,128)} %copy-done.1) | copy-start | bytes 1572868
  281.5 5.8 %collective-permute-start.12 = (f32[32,1,4,128]{3,0,2,1:T(8,128)}, f32[32,1,4,128]{3,0,2,1:T(8,128)S(1)}, u32[]{:S(2)}, u32[]{:S(2)}) collective-permute-start(f32[32,1,4,128]{3,0,2,1:T(8,128)} %get-tuple-element.28), channel_id=1, source_target_pairs={{0,2},{2,4},{4,6},{6,8},{8,10},{10,12},{12,14},{1,3},{3,5},{5,7},{... | collective-permute-start | bytes 196616 | tf_op jit(solution)/shard_map/ppermute | solution.py:22
  285.9 12.6 %copy-start.9 = (f32[2,4,128,128]{2,3,1,0:T(8,128)S(1)}, f32[2,4,128,128]{2,3,1,0:T(8,128)}, u32[]{:S(2)}) copy-start(f32[2,4,128,128]{2,3,1,0:T(8,128)} %copy-done.7) | copy-start | bytes 1572868
  285.9 6.5 %collective-permute-start.13 = (f32[32,1,4,128]{3,0,2,1:T(8,128)}, f32[32,1,4,128]{3,0,2,1:T(8,128)S(1)}, u32[]{:S(2)}, u32[]{:S(2)}) collective-permute-start(f32[32,1,4,128]{3,0,2,1:T(8,128)} %get-tuple-element.27), channel_id=1, source_target_pairs={{2,0},{4,2},{6,4},{8,6},{10,8},{12,10},{14,12},{3,1},{5,3},{7,5},{... | collective-permute-start | bytes 196616 | tf_op jit(solution)/shard_map/ppermute | solution.py:23
  292.4 6.6 %collective-permute-start.15 = (f32[32,4,1,128]{3,0,2,1:T(8,128)S(1)}, f32[32,4,1,128]{3,0,2,1:T(8,128)S(1)}, u32[]{:S(2)}, u32[]{:S(2)}) collective-permute-start(f32[32,4,1,128]{3,0,2,1:T(8,128)S(1)} %get-tuple-element.22), channel_id=1, source_target_pairs={{1,0},{3,2},{5,4},{7,6},{9,8},{11,10},{13,12},{15,14},{17,16},{19,... | collective-permute-start | bytes 196616 | tf_op jit(solution)/shard_map/ppermute | solution.py:23
  293.7 4.2 %collective-permute-start.14 = (f32[32,4,1,128]{3,0,2,1:T(8,128)S(1)}, f32[32,4,1,128]{3,0,2,1:T(8,128)S(1)}, u32[]{:S(2)}, u32[]{:S(2)}) collective-permute-start(f32[32,4,1,128]{3,0,2,1:T(8,128)S(1)} %get-tuple-element.21), channel_id=1, source_target_pairs={{0,1},{2,3},{4,5},{6,7},{8,9},{10,11},{12,13},{14,15},{16,17},{18,... | collective-permute-start | bytes 196616 | tf_op jit(solution)/shard_map/ppermute | solution.py:22
  297.3 2.3 copy-start.6
  297.9 2.3 copy-start.10
where the time goes:
time: 368 us
  blocking collectives  178 us (48%)
  waiting for transfers between devices  86.4 us (23%)
  starting transfers between devices  38 us (10%)
  other arithmetic  29.3 us (8%)
  matrix products  25.8 us (7%)
  local copies, waits for them, and re-layouts  9.52 us (3%)
    psum x3, blocking collectives, body(): lower_factor = jnp.linalg.cholesky(lax.psum(partial_gram, ('row', 'col')))  178 us
    ppermute x8, waiting for transfers between devices, padded_2(): before = lax.ppermute(last, axis, up)  50.7 us
    all_to_all x1, waiting for transfers between devices, body(): lax.all_to_all(placed, 'row', split_axis=0, concat_axis=1, tiled=True)  29 us
    ppermute x8, starting transfers between devices, padded_2(): before = lax.ppermute(last, axis, up)  19.9 us
    dot_general x27, matrix products, propagate(): jnp.einsum('abij,kabj->kabi', tiles[offset], shifted, precision=lax.Preci...  16.7 us
    another operation x9, other arithmetic, body(): lower_factor = jnp.linalg.cholesky(lax.psum(partial_gram, ('row', 'col')))  10.8 us
    ppermute x8, starting transfers between devices, padded_2(): after = lax.ppermute(leading, axis, down)  10.7 us
    another operation x6, other arithmetic, solve_lower(): jax.scipy.linalg.solve_triangular(lower_factor, flat, lower=True)  9.78 us
  transfers between devices with their start and end apart: 17, of which 6 were waited for; matrix products, arithmetic and copies ran while one was open for 6% of the time, Pallas kernels for 0%

commit v1 on v0

v1 whole, which is shorter than its diff:
```python
import functools
import math

import jax
import jax.numpy as jnp
from jax import lax
from jax.experimental import pallas as pl
from jax.experimental.pallas import tpu as pltpu
from jax.sharding import PartitionSpec as P

ITERS = 3
SHARPNESS = 4.0
EPSILON = 1e-06
HIGHEST = lax.Precision.HIGHEST
F32 = jnp.float32
BF16 = jnp.bfloat16
LANES = 128
STEPS = ((-1, 0), (1, 0), (0, -1), (0, 1), (-1, -1), (-1, 1), (1, -1), (1, 1))


def whiten(gram):
    k = gram.shape[0]
    rows = lax.broadcasted_iota(jnp.int32, (k, k), 0)
    cols = lax.broadcasted_iota(jnp.int32, (k, k), 1)
    eye = (rows == cols).astype(F32)
    work = jnp.concatenate([gram, eye], axis=1)
    at = lax.broadcasted_iota(jnp.int32, (k, 1), 0)
    for step in range(k - 1):
        pivot = work[step : step + 1, :]
        pivot = pivot / pivot[:, step : step + 1]
        below = jnp.where(at > step, work[:, step : step + 1], 0.0)
        work = work - below * pivot
    diag = jnp.sum(work[:, :k] * eye, axis=1, keepdims=True)
    return work[:, k:] / jnp.sqrt(diag)


def kernel(
    rows_n, cols_n, th, nb, sw, scale,
    feat_ref, seq_ref, link_ref, start_ref, out_ref,
    unit, placed, land, fpad, thi, tlo, deg, vpad, grown, gsend, grecv,
    a2a_send, a2a_recv, halo_send, halo_recv, gram_send, gram_recv,
):
    row, col = lax.axis_index("row"), lax.axis_index("col")
    peers = rows_n * cols_n
    me = row * cols_n + col
    tokens, width = feat_ref.shape
    vec_n = start_ref.shape[0]
    bw = LANES
    blocks = th * nb
    chunk = th * sw
    per = LANES // chunk
    supers = tokens // LANES

    def at(peer):
        return {"row": peer // cols_n, "col": lax.rem(peer, cols_n)}

    def exists(dr, dc):
        r, c = row + dr, col + dc
        return (r >= 0) & (r < rows_n) & (c >= 0) & (c < cols_n)

    def piece(buf, dr, dc, arriving):
        def pick(step, n):
            if step == 0:
                return pl.ds(1, n)
            if arriving:
                return pl.ds(n + 1 if step < 0 else 0, 1)
            return pl.ds(1 if step < 0 else n, 1)

        return buf.at[pick(dr, th), pick(dc, nb)]

    def halo_copy(buf, stage, way, sending):
        dr, dc = STEPS[way]
        r = row + dr if sending else row - dr
        c = col + dc if sending else col - dc
        return pltpu.make_async_remote_copy(
            src_ref=piece(buf, dr, dc, False),
            dst_ref=piece(buf, dr, dc, True),
            send_sem=halo_send.at[stage, way],
            recv_sem=halo_recv.at[stage, way],
            device_id={"row": r, "col": c},
            device_id_type=pl.DeviceIdType.MESH,
        )

    def halo_start(buf, stage):
        for way, (dr, dc) in enumerate(STEPS):
            @pl.when(exists(dr, dc))
            def _():
                halo_copy(buf, stage, way, True).start()

    def halo_wait(buf, stage, ways=range(8)):
        for way in ways:
            dr, dc = STEPS[way]

            @pl.when(exists(-dr, -dc))
            def _():
                halo_copy(buf, stage, way, False).wait_recv()

    def halo_finish(buf, stage):
        for way, (dr, dc) in enumerate(STEPS):
            @pl.when(exists(dr, dc))
            def _():
                halo_copy(buf, stage, way, True).wait_send()

    def halo_zero(buf):
        for dr, dc in STEPS:
            @pl.when(jnp.logical_not(exists(-dr, -dc)))
            def _():
                where = piece(buf, dr, dc, True)
                where[...] = jnp.zeros(where.shape, where.dtype)

    barrier = pltpu.get_barrier_semaphore()

    @pl.loop(1, peers)
    def _(step):
        pl.semaphore_signal(
            barrier, inc=1, device_id=at(lax.rem(me + step, peers)),
            device_id_type=pl.DeviceIdType.MESH,
        )

    for y in range(th):
        for x in range(nb):
            lo = (y * nb + x) * bw
            vpad[0, 1 + y, 1 + x] = start_ref[:, lo : lo + bw]
    for step in range(ITERS):
        halo_zero(vpad.at[step])
    halo_zero(fpad)
    deg[...] = jnp.zeros_like(deg)

    @pl.loop(0, tokens // 64)
    def _(step):
        rows = pl.ds(pl.multiple_of(step * 64, 64), 64)
        wide = feat_ref[rows, :].astype(F32)
        squares = jnp.sum(wide * wide, axis=1, keepdims=True)
        unit[rows, :] = (wide * lax.rsqrt(squares + EPSILON)).astype(BF16)

    pl.semaphore_wait(barrier, peers - 1)
    halo_start(vpad.at[0], 0)

    def strip_copy(index, part, dest, source):
        return pltpu.make_async_remote_copy(
            src_ref=placed.at[index, pl.ds(part * chunk, chunk)],
            dst_ref=land.at[source],
            send_sem=a2a_send.at[dest],
            recv_sem=a2a_recv.at[source],
            device_id={"row": dest},
            device_id_type=pl.DeviceIdType.MESH,
        )

    @pl.loop(0, supers)
    def _(step):
        index = lax.rem(row // per + 1 + step, supers)
        order = seq_ref[:, pl.ds(pl.multiple_of(index * LANES, LANES), LANES)]
        order = jnp.broadcast_to(order.astype(F32), (LANES, LANES)).T
        lane = lax.broadcasted_iota(jnp.int32, (LANES, LANES), 1).astype(F32)
        chosen = jnp.concatenate(
            [
                jnp.where(order == lane + float(j * LANES), 1.0, 0.0).astype(BF16)
                for j in range(supers)
            ],
            axis=1,
        )
        placed[index] = jnp.dot(chosen, unit[...], preferred_element_type=F32).astype(BF16)
        for part in range(per):
            dest = index * per + part

            @pl.when(dest != row)
            def _():
                strip_copy(index, part, dest, row).start()

            @pl.when(dest == row)
            def _():
                land[dest] = placed[index, pl.ds(part * chunk, chunk)]

    group = max(1, 16 // sw)
    span = group * sw
    in_block = bw // span

    @pl.loop(0, rows_n // group)
    def _(step):
        first = lax.rem(row // group + step, rows_n // group)
        for i in range(group):
            source = first * group + i

            @pl.when(source != row)
            def _():
                strip_copy(0, 0, row, source).wait_recv()

        rows = pl.ds(pl.multiple_of(lax.rem(first, in_block) * span, span), span)
        x = 1 + first // in_block
        if group == 1:
            for y in range(th):
                fpad[1 + y, x, rows, :] = land[first, y * sw : (y + 1) * sw, :]
        else:
            wide = [land[first * group + i].astype(F32) for i in range(group)]
            for y in range(th):
                joined = jnp.concatenate([w[y * sw : (y + 1) * sw] for w in wide], axis=0)
                fpad[1 + y, x, rows, :] = joined.astype(BF16)

    halo_start(fpad, ITERS)

    def tile(y, x, dy, dx):
        offset = (dy + 1) * 3 + dx + 1
        block = y * nb + x
        near = fpad[1 + y + dy, 1 + x + dx]
        own = fpad[1 + y, 1 + x]
        dots = lax.dot_general(
            near, own, (((1,), (1,)), ((), ())), preferred_element_type=F32
        )
        at_row, at_col = row * th + y + dy, col * nb + x + dx
        inside = (at_row >= 0) & (at_row < rows_n * th)
        inside &= (at_col >= 0) & (at_col < cols_n * nb)
        if offset != 4:
            inside &= link_ref[offset * blocks + block] == 1
        link = jnp.where(inside, 1.0, 0.0).astype(F32)
        value = jnp.exp(SHARPNESS * (dots - 1.0)) * link
        deg[block] += jnp.sum(value, axis=0, keepdims=True)
        high = value.astype(BF16)
        thi[block, offset * bw : (offset + 1) * bw, :] = high
        tlo[block, offset * bw : (offset + 1) * bw, :] = (value - high.astype(F32)).astype(BF16)

    def tiles(y, dy):
        @pl.loop(0, nb)
        def _(x):
            tile(y, x, dy, 0)

        @pl.loop(1, nb)
        def _(x):
            tile(y, x, dy, -1)
            tile(y, x - 1, dy, 1)

    def side_tiles(y, dy):
        tile(y, 0, dy, -1)
        tile(y, nb - 1, dy, 1)

    inner = [(y, dy) for y in range(th) for dy in (-1, 0, 1) if 0 <= y + dy < th]
    for y, dy in inner:
        tiles(y, dy)
    halo_wait(fpad, ITERS, (2, 3))
    for y, dy in inner:
        side_tiles(y, dy)
    for edge, ways in (((0, -1), (1, 6, 7)), ((th - 1, 1), (0, 4, 5))):
        halo_wait(fpad, ITERS, ways)
        tiles(*edge)
        side_tiles(*edge)
    deg[...] = 1.0 / deg[...]

    def gram_copy(stage, dest, source):
        return pltpu.make_async_remote_copy(
            src_ref=gsend.at[stage],
            dst_ref=grecv.at[stage, source],
            send_sem=gram_send.at[stage, dest],
            recv_sem=gram_recv.at[stage, source],
            device_id=at(dest),
            device_id_type=pl.DeviceIdType.MESH,
        )

    pack = LANES // vec_n
    part_rows = vec_n // pack
    inverse = None
    for step in range(ITERS):
        halo_wait(vpad.at[step], step)

        @pl.loop(0, blocks)
        def _(block):
            y, x = block // nb, lax.rem(block, nb)
            field = jnp.concatenate(
                [vpad[step, y + o // 3, x + o % 3] for o in range(9)], axis=1
            )
            high = field.astype(BF16)
            low = (field - high.astype(F32)).astype(BF16)
            both = jnp.dot(
                jnp.concatenate([high, low], axis=0), thi[block], preferred_element_type=F32
            )
            total = both[:vec_n] + both[vec_n:]
            total += jnp.dot(high, tlo[block], preferred_element_type=F32)
            grown[:, pl.ds(pl.multiple_of(block * bw, bw), bw)] = total * deg[block]

        value = grown[...]
        if step:
            total = jnp.zeros((part_rows, LANES), F32)
            last = step - 1

            def add(source, total):
                @pl.when(source != me)
                def _():
                    gram_copy(last, me, source).wait_recv()

                return total + grecv[last, source]

            total = lax.fori_loop(0, peers, add, total)
            gram = jnp.concatenate(
                [total[:, i * vec_n : (i + 1) * vec_n] for i in range(pack)], axis=0
            )
            inverse = whiten(gram)
            value = jnp.dot(inverse, value, precision=HIGHEST, preferred_element_type=F32)
            grown[...] = value
        if step + 1 < ITERS:
            for y in range(th):
                for x in range(nb):
                    lo = (y * nb + x) * bw
                    vpad[step + 1, 1 + y, 1 + x] = value[:, lo : lo + bw]
            halo_start(vpad.at[step + 1], step + 1)
        gram = lax.dot_general(
            value, value, (((1,), (1,)), ((), ())),
            precision=HIGHEST, preferred_element_type=F32,
        )
        packed = jnp.concatenate(
            [gram[i * part_rows : (i + 1) * part_rows] for i in range(pack)], axis=1
        )
        gsend[step] = packed
        grecv[step, me] = packed

        @pl.loop(1, peers)
        def _(other):
            gram_copy(step, lax.rem(me + other, peers), me).start()

    def add(source, total):
        @pl.when(source != me)
        def _():
            gram_copy(ITERS - 1, me, source).wait_recv()

        return total + grecv[ITERS - 1, source]

    total = lax.fori_loop(0, peers, add, jnp.zeros((part_rows, LANES), F32))
    gram = jnp.concatenate(
        [total[:, i * vec_n : (i + 1) * vec_n] for i in range(pack)], axis=0
    )
    out_ref[...] = jnp.dot(
        whiten(gram), grown[...], precision=HIGHEST, preferred_element_type=F32
    ) * scale

    for step in range(ITERS):
        halo_finish(vpad.at[step], step)

        @pl.loop(1, peers)
        def _(other):
            gram_copy(step, lax.rem(me + other, peers), me).wait_send()

    halo_finish(fpad, ITERS)

    @pl.loop(0, rows_n)
    def _(dest):
        @pl.when(dest != row)
        def _():
            strip_copy(0, 0, dest, row).wait_send()


def body(features, seq_order, block_links, start_vectors):
    rows_n = lax.axis_size("row")
    cols_n = lax.axis_size("col")
    tokens, width = features.shape
    vec_n, th, tile_w = start_vectors.shape
    nb = block_links.shape[2]
    sw = tile_w // rows_n
    bw = tile_w // nb
    peers = rows_n * cols_n
    blocks = th * nb
    scale = math.sqrt(th * rows_n * tile_w * cols_n)
    part_rows = vec_n * vec_n // LANES
    vmem = pl.BlockSpec(memory_space=pltpu.VMEM)
    dma = pltpu.SemaphoreType.DMA
    out = pl.pallas_call(
        functools.partial(kernel, rows_n, cols_n, th, nb, sw, scale),
        out_shape=jax.ShapeDtypeStruct((vec_n, tokens), F32),
        in_specs=[vmem, vmem, pl.BlockSpec(memory_space=pltpu.SMEM), vmem],
        out_specs=vmem,
        scratch_shapes=[
            pltpu.VMEM((tokens, width), BF16),
            pltpu.VMEM((tokens // LANES, LANES, width), BF16),
            pltpu.VMEM((rows_n, th * sw, width), BF16),
            pltpu.VMEM((th + 2, nb + 2, bw, width), BF16),
            pltpu.VMEM((blocks, 9 * bw, bw), BF16),
            pltpu.VMEM((blocks, 9 * bw, bw), BF16),
            pltpu.VMEM((blocks, 1, bw), F32),
            pltpu.VMEM((ITERS, th + 2, nb + 2, vec_n, bw), F32),
            pltpu.VMEM((vec_n, tokens), F32),
            pltpu.VMEM((ITERS, part_rows, LANES), F32),
            pltpu.VMEM((ITERS, peers, part_rows, LANES), F32),
            dma((rows_n,)),
            dma((rows_n,)),
            dma((ITERS + 1, len(STEPS))),
            dma((ITERS + 1, len(STEPS))),
            dma((ITERS, peers)),
            dma((ITERS, peers)),
        ],
        compiler_params=pltpu.CompilerParams(
            collective_id=0, has_side_effects=True, vmem_limit_bytes=48 * 2**20
        ),
    )(features, seq_order, block_links.reshape(-1), start_vectors.reshape(vec_n, tokens))
    return out.reshape(vec_n, th, tile_w)


def solution(mesh):
    return jax.shard_map(
        body,
        mesh=mesh,
        in_specs=(
            P(("slide", "row", "col"), None),
            P(("slide", "row", "col"), None),
            P(None, ("slide", "row"), "col"),
            P(None, ("slide", "row"), "col"),
        ),
        out_specs=P(None, ("slide", "row"), "col"),
        check_vma=False,
    )
```

time: 368 us -> 154 us (0.42)
  blocking collectives: 178 us -> 0 us
  Pallas kernels: 0 us -> 148 us
  waiting for transfers between devices: 86.4 us -> 0 us
  starting transfers between devices: 38 us -> 0 us
  other arithmetic: 29.3 us -> 0 us
  matrix products: 25.8 us -> 0 us
  local copies, waits for them, and re-layouts: 9.52 us -> 4.84 us
    psum x3 -> x0, blocking collectives: 178 us -> none  [body(): lower_factor = jnp.linalg.cholesky(lax.psum(partial_gram, ('row', 'col')))]
    pallas_call x0 -> x1, Pallas kernels: none -> 148 us  [body(): pl.pallas_call(functools.partial(kernel, rows_n, cols_n, th, nb, sw, scal...]
    ppermute x16 -> x0, waiting for transfers between devices: 57.4 us -> none  [the longest x8 50.7 us: padded_2(): before = lax.ppermute(last, axis, up)]
    ppermute x16 -> x0, starting transfers between devices: 30.6 us -> none  [the longest x8 19.9 us: padded_2(): before = lax.ppermute(last, axis, up)]
    all_to_all x1 -> x0, waiting for transfers between devices: 29 us -> none  [body(): lax.all_to_all(placed, 'row', split_axis=0, concat_axis=1, tiled=True)]
    dot_general x39 -> x0, matrix products: 24.1 us -> none  [the longest x27 16.7 us: propagate(): jnp.einsum('abij,kabj->kabi', tiles[offset], shifted, precision=lax.Preci...]
    another operation x15 -> x0, other arithmetic: 20.6 us -> none  [the longest x9 10.8 us: body(): lower_factor = jnp.linalg.cholesky(lax.psum(partial_gram, ('row', 'col')))]
    all_to_all x1 -> x0, starting transfers between devices: 7.41 us -> none  [body(): lax.all_to_all(placed, 'row', split_axis=0, concat_axis=1, tiled=True)]
  transfers between devices with their start and end apart: 17 -> 0, of which waited for: 6 -> 0; matrix products, arithmetic and copies ran while one was open for 6% -> 0% of each run, Pallas kernels for 0% -> 0%
where the time goes in v1:
time: 154 us; the launch traced here: 153 us
  Pallas kernels  148 us (96%)
  local copies, waits for them, and re-layouts  4.84 us (3%)
    pallas_call x1, Pallas kernels, body(): pl.pallas_call(functools.partial(kernel, rows_n, cols_n, th, nb, sw, scal...  148 us
    unnamed x6, local copies, waits for them, and re-layouts  3.99 us

profile of v1, /device:TPU:0, one launch (start us, length us, event | category | flops | bytes accessed | tf_op | source)
XLA Modules:
  0.0 153.4 jit_solution(9927272245371000948)
XLA Ops:
  0.0 0.8 copy.6
  0.8 0.1 reshape.9.link_ref
  0.9 0.9 copy.7
  1.8 0.0 copy-start
  1.8 1.6 %copy-done = bf16[1024,1024]{1,0:T(8,128)(2,1)S(1)} copy-done((bf16[1024,1024]{1,0:T(8,128)(2,1)S(1)}, bf16[1024,1024]{1,0:T(8,128)(2,1)}, u32[]{:S(2)}) %copy-start) | copy-done | bytes 2097176
  3.4 0.0 copy-start.1
  3.4 0.7 copy-done.1
  4.1 148.5 %shard_map.46 = f32[32,1024]{1,0:T(8,128)S(1)} custom-call(bf16[1024,1024]{1,0:T(8,128)(2,1)S(1)} %copy-done, s32[1,1024]{1,0:T(1,128)S(1)} %copy-done.1, s32[72]{0:T(128)S(1)} %reshape.9.link_ref, f32[32,1024]{1,0:T(8,128)S(1)} %bitcast.2), custom_call_target="tpu_custom_call" | custom-call | tf_op jit(solution)/shard_map/pallas_call | solution.py:362
  152.6 0.8 reshape.11
Async XLA Ops:
  1.8 1.6 %copy-start = (bf16[1024,1024]{1,0:T(8,128)(2,1)S(1)}, bf16[1024,1024]{1,0:T(8,128)(2,1)}, u32[]{:S(2)}) copy-start(bf16[1024,1024]{1,0:T(8,128)(2,1)} %feat_ref.1) | copy-start | bytes 6291460
  3.4 0.7 copy-start.1

commit v2 on v1

--- a/solution.py
+++ b/solution.py
@@ -16,6 +16,13 @@
 BF16 = jnp.bfloat16
 LANES = 128
 STEPS = ((-1, 0), (1, 0), (0, -1), (0, 1), (-1, -1), (-1, 1), (1, -1), (1, 1))
+
+
+def snake(place, rows_n):
+    if rows_n % 4:
+        return place
+    odd_pair = lax.rem(place // 2, 2)
+    return place + odd_pair * (1 - 2 * lax.rem(place, 2))
 
 
 def whiten(gram):
@@ -38,11 +45,14 @@
     rows_n, cols_n, th, nb, sw, scale,
     feat_ref, seq_ref, link_ref, start_ref, out_ref,
     unit, placed, land, fpad, thi, tlo, deg, vpad, grown, gsend, grecv,
-    a2a_send, a2a_recv, halo_send, halo_recv, gram_send, gram_recv,
+    begun, linked, swapped,
+    a2a_send, a2a_recv, halo_send, halo_recv, gram_send, gram_recv, swap_send, swap_recv,
 ):
     row, col = lax.axis_index("row"), lax.axis_index("col")
     peers = rows_n * cols_n
     me = row * cols_n + col
+    trow = snake(row, rows_n)
+    moved = trow != row
     tokens, width = feat_ref.shape
     vec_n = start_ref.shape[0]
     bw = LANES
@@ -55,7 +65,7 @@
         return {"row": peer // cols_n, "col": lax.rem(peer, cols_n)}
 
     def exists(dr, dc):
-        r, c = row + dr, col + dc
+        r, c = trow + dr, col + dc
         return (r >= 0) & (r < rows_n) & (c >= 0) & (c < cols_n)
 
     def piece(buf, dr, dc, arriving):
@@ -70,7 +80,7 @@
 
     def halo_copy(buf, stage, way, sending):
         dr, dc = STEPS[way]
-        r = row + dr if sending else row - dr
+        r = snake(trow + dr if sending else trow - dr, rows_n)
         c = col + dc if sending else col - dc
         return pltpu.make_async_remote_copy(
             src_ref=piece(buf, dr, dc, False),
@@ -81,8 +91,10 @@
             device_id_type=pl.DeviceIdType.MESH,
         )
 
-    def halo_start(buf, stage):
-        for way, (dr, dc) in enumerate(STEPS):
+    def halo_start(buf, stage, ways=range(8)):
+        for way in ways:
+            dr, dc = STEPS[way]
+
             @pl.when(exists(dr, dc))
             def _():
                 halo_copy(buf, stage, way, True).start()
@@ -95,11 +107,48 @@
             def _():
                 halo_copy(buf, stage, way, False).wait_recv()
 
-    def halo_finish(buf, stage):
-        for way, (dr, dc) in enumerate(STEPS):
+    def halo_finish(buf, stage, ways=range(8)):
+        for way in ways:
+            dr, dc = STEPS[way]
+
             @pl.when(exists(dr, dc))
             def _():
                 halo_copy(buf, stage, way, True).wait_send()
+
+    def corner_copy(way):
+        dr, dc = STEPS[way]
+        edge = pl.ds(th + 1 if dr < 0 else 0, 1)
+        return pltpu.make_async_remote_copy(
+            src_ref=fpad.at[edge, pl.ds(1 if dc < 0 else nb, 1)],
+            dst_ref=fpad.at[edge, pl.ds(nb + 1 if dc < 0 else 0, 1)],
+            send_sem=halo_send.at[ITERS, way],
+            recv_sem=halo_recv.at[ITERS, way],
+            device_id={"col": col + dc},
+            device_id_type=pl.DeviceIdType.MESH,
+        )
+
+    def corner_when(way, action):
+        dr, dc = STEPS[way]
+
+        @pl.when(exists(-dr, dc))
+        def _():
+            action(corner_copy(way))
+
+    def swap_copy(src, dst, index):
+        return pltpu.make_async_remote_copy(
+            src_ref=src,
+            dst_ref=dst,
+            send_sem=swap_send.at[index],
+            recv_sem=swap_recv.at[index],
+            device_id={"row": trow},
+            device_id_type=pl.DeviceIdType.MESH,
+        )
+
+    swaps = (
+        (start_ref, begun, 0),
+        (link_ref, linked, 1),
+        (grown, swapped, 2),
+    )
 
     def halo_zero(buf):
         for dr, dc in STEPS:
@@ -117,10 +166,6 @@
             device_id_type=pl.DeviceIdType.MESH,
         )
 
-    for y in range(th):
-        for x in range(nb):
-            lo = (y * nb + x) * bw
-            vpad[0, 1 + y, 1 + x] = start_ref[:, lo : lo + bw]
     for step in range(ITERS):
         halo_zero(vpad.at[step])
     halo_zero(fpad)
@@ -134,7 +179,16 @@
         unit[rows, :] = (wide * lax.rsqrt(squares + EPSILON)).astype(BF16)
 
     pl.semaphore_wait(barrier, peers - 1)
-    halo_start(vpad.at[0], 0)
+
+    @pl.when(moved)
+    def _():
+        for swap in swaps[:2]:
+            swap_copy(*swap).start()
+
+    @pl.when(jnp.logical_not(moved))
+    def _():
+        begun[...] = start_ref[...]
+        linked[...] = link_ref[...]
 
     def strip_copy(index, part, dest, source):
         return pltpu.make_async_remote_copy(
@@ -142,13 +196,13 @@
             dst_ref=land.at[source],
             send_sem=a2a_send.at[dest],
             recv_sem=a2a_recv.at[source],
-            device_id={"row": dest},
+            device_id={"row": snake(dest, rows_n)},
             device_id_type=pl.DeviceIdType.MESH,
         )
 
     @pl.loop(0, supers)
     def _(step):
-        index = lax.rem(row // per + 1 + step, supers)
+        index = lax.rem(trow // per + 1 + step, supers)
         order = seq_ref[:, pl.ds(pl.multiple_of(index * LANES, LANES), LANES)]
         order = jnp.broadcast_to(order.astype(F32), (LANES, LANES)).T
         lane = lax.broadcasted_iota(jnp.int32, (LANES, LANES), 1).astype(F32)
@@ -163,13 +217,24 @@
         for part in range(per):
             dest = index * per + part
 
-            @pl.when(dest != row)
+            @pl.when(dest != trow)
             def _():
                 strip_copy(index, part, dest, row).start()
 
-            @pl.when(dest == row)
-            def _():
-                land[dest] = placed[index, pl.ds(part * chunk, chunk)]
+            @pl.when(dest == trow)
+            def _():
+                land[row] = placed[index, pl.ds(part * chunk, chunk)]
+
+    @pl.when(moved)
+    def _():
+        for swap in swaps[:2]:
+            swap_copy(*swap).wait()
+
+    for y in range(th):
+        for x in range(nb):
+            lo = (y * nb + x) * bw
+            vpad[0, 1 + y, 1 + x] = begun[:, lo : lo + bw]
+    halo_start(vpad.at[0], 0)
 
     group = max(1, 16 // sw)
     span = group * sw
@@ -183,7 +248,7 @@
 
             @pl.when(source != row)
             def _():
-                strip_copy(0, 0, row, source).wait_recv()
+                strip_copy(0, 0, trow, source).wait_recv()
 
         rows = pl.ds(pl.multiple_of(lax.rem(first, in_block) * span, span), span)
         x = 1 + first // in_block
@@ -196,7 +261,7 @@
                 joined = jnp.concatenate([w[y * sw : (y + 1) * sw] for w in wide], axis=0)
                 fpad[1 + y, x, rows, :] = joined.astype(BF16)
 
-    halo_start(fpad, ITERS)
+    halo_start(fpad, ITERS, range(4))
 
     def tile(y, x, dy, dx):
         offset = (dy + 1) * 3 + dx + 1
@@ -206,12 +271,12 @@
         dots = lax.dot_general(
             near, own, (((1,), (1,)), ((), ())), preferred_element_type=F32
         )
-        at_row, at_col = row * th + y + dy, col * nb + x + dx
+        at_row, at_col = trow * th + y + dy, col * nb + x + dx
         inside = (at_row >= 0) & (at_row < rows_n * th)
         inside &= (at_col >= 0) & (at_col < cols_n * nb)
+        link = jnp.where(inside, 1.0, 0.0).astype(F32)
         if offset != 4:
-            inside &= link_ref[offset * blocks + block] == 1
-        link = jnp.where(inside, 1.0, 0.0).astype(F32)
+            link = link * linked[offset * blocks + block]
         value = jnp.exp(SHARPNESS * (dots - 1.0)) * link
         deg[block] += jnp.sum(value, axis=0, keepdims=True)
         high = value.astype(BF16)
@@ -238,9 +303,14 @@
     halo_wait(fpad, ITERS, (2, 3))
     for y, dy in inner:
         side_tiles(y, dy)
-    for edge, ways in (((0, -1), (1, 6, 7)), ((th - 1, 1), (0, 4, 5))):
-        halo_wait(fpad, ITERS, ways)
+    edges = (((0, -1), 1, (6, 7)), ((th - 1, 1), 0, (4, 5)))
+    for edge, way, corners in edges:
+        halo_wait(fpad, ITERS, (way,))
+        for corner in corners:
+            corner_when(corner, lambda copy: copy.start())
         tiles(*edge)
+    for edge, way, corners in edges:
+        halo_wait(fpad, ITERS, corners)
         side_tiles(*edge)
     deg[...] = 1.0 / deg[...]
 
@@ -314,6 +384,15 @@
         def _(other):
             gram_copy(step, lax.rem(me + other, peers), me).start()
 
+        if step + 1 == ITERS:
+            @pl.when(moved)
+            def _():
+                swap_copy(*swaps[2]).start()
+
+            @pl.when(jnp.logical_not(moved))
+            def _():
+                swapped[...] = value
+
     def add(source, total):
         @pl.when(source != me)
         def _():
@@ -325,8 +404,14 @@
     gram = jnp.concatenate(
         [total[:, i * vec_n : (i + 1) * vec_n] for i in range(pack)], axis=0
     )
+    inverse = whiten(gram)
+
+    @pl.when(moved)
+    def _():
+        swap_copy(*swaps[2]).wait()
+
     out_ref[...] = jnp.dot(
-        whiten(gram), grown[...], precision=HIGHEST, preferred_element_type=F32
+        inverse, swapped[...], precision=HIGHEST, preferred_element_type=F32
     ) * scale
 
     for step in range(ITERS):
@@ -336,11 +421,13 @@
         def _(other):
             gram_copy(step, lax.rem(me + other, peers), me).wait_send()
 
-    halo_finish(fpad, ITERS)
+    halo_finish(fpad, ITERS, range(4))
+    for way in range(4, 8):
+        corner_when(way, lambda copy: copy.wait_send())
 
     @pl.loop(0, rows_n)
     def _(dest):
-        @pl.when(dest != row)
+        @pl.when(dest != trow)
         def _():
             strip_copy(0, 0, dest, row).wait_send()
 
@@ -357,12 +444,14 @@
     blocks = th * nb
     scale = math.sqrt(th * rows_n * tile_w * cols_n)
     part_rows = vec_n * vec_n // LANES
+    links = (block_links == 1).astype(F32).reshape(9 * blocks, 1, 1)
+    links = jnp.broadcast_to(links, (9 * blocks, 1, LANES))
     vmem = pl.BlockSpec(memory_space=pltpu.VMEM)
     dma = pltpu.SemaphoreType.DMA
     out = pl.pallas_call(
         functools.partial(kernel, rows_n, cols_n, th, nb, sw, scale),
         out_shape=jax.ShapeDtypeStruct((vec_n, tokens), F32),
-        in_specs=[vmem, vmem, pl.BlockSpec(memory_space=pltpu.SMEM), vmem],
+        in_specs=[vmem] * 4,
         out_specs=vmem,
         scratch_shapes=[
             pltpu.VMEM((tokens, width), BF16),
@@ -376,17 +465,22 @@
             pltpu.VMEM((vec_n, tokens), F32),
             pltpu.VMEM((ITERS, part_rows, LANES), F32),
             pltpu.VMEM((ITERS, peers, part_rows, LANES), F32),
+            pltpu.VMEM((vec_n, tokens), F32),
+            pltpu.VMEM((9 * blocks, 1, LANES), F32),
+            pltpu.VMEM((vec_n, tokens), F32),
             dma((rows_n,)),
             dma((rows_n,)),
             dma((ITERS + 1, len(STEPS))),
             dma((ITERS + 1, len(STEPS))),
             dma((ITERS, peers)),
             dma((ITERS, peers)),
+            dma((3,)),
+            dma((3,)),
         ],
         compiler_params=pltpu.CompilerParams(
             collective_id=0, has_side_effects=True, vmem_limit_bytes=48 * 2**20
         ),
-    )(features, seq_order, block_links.reshape(-1), start_vectors.reshape(vec_n, tokens))
+    )(features, seq_order, links, start_vectors.reshape(vec_n, tokens))
     return out.reshape(vec_n, th, tile_w)
 
 

time: 154 us -> 117 us (0.76)
  Pallas kernels: 148 us -> 112 us
    pallas_call x1, Pallas kernels: 148 us -> 112 us  [body(): pl.pallas_call(functools.partial(kernel, rows_n, cols_n, th, nb, sw, scal...]
    unnamed x6 -> x5, local copies, waits for them, and re-layouts: 3.99 us -> 3.21 us
where the time goes in v2:
time: 117 us
  Pallas kernels  112 us (96%)
  local copies, waits for them, and re-layouts  4.31 us (4%)
    pallas_call x1, Pallas kernels, body(): pl.pallas_call(functools.partial(kernel, rows_n, cols_n, th, nb, sw, scal...  112 us
    unnamed x5, local copies, waits for them, and re-layouts  3.21 us

profile of v2, /device:TPU:0, one launch (start us, length us, event | category | flops | bytes accessed | tf_op | source)
XLA Modules:
  0.0 117.2 jit_solution(14231508064301918098)
XLA Ops:
  0.0 0.7 compare_convert_fusion
  0.7 0.1 copy.6
  0.8 0.1 reshape.13
  0.9 0.1 broadcast_in_dim.11.link_ref
  1.0 0.9 copy.7
  2.0 0.0 copy-start
  2.0 1.6 %copy-done = bf16[1024,1024]{1,0:T(8,128)(2,1)S(1)} copy-done((bf16[1024,1024]{1,0:T(8,128)(2,1)S(1)}, bf16[1024,1024]{1,0:T(8,128)(2,1)}, u32[]{:S(2)}) %copy-start) | copy-done | bytes 2097176
  3.6 0.0 copy-start.1
  3.6 0.7 copy-done.1
  4.3 112.1 %shard_map.46 = f32[32,1024]{1,0:T(8,128)S(1)} custom-call(bf16[1024,1024]{1,0:T(8,128)(2,1)S(1)} %copy-done, s32[1,1024]{1,0:T(1,128)S(1)} %copy-done.1, f32[72,1,128]{2,1,0:T(1,128)S(1)} %broadcast_in_dim.11.link_ref, f32[32,1024]{1,0:T(8,128)S(1)} %bitcast.2), custom_call_target="tpu_custom_call" | custom-call | tf_op jit(solution)/shard_map/pallas_call | solution.py:451
  116.4 0.8 reshape.12
Async XLA Ops:
  2.0 1.6 %copy-start = (bf16[1024,1024]{1,0:T(8,128)(2,1)S(1)}, bf16[1024,1024]{1,0:T(8,128)(2,1)}, u32[]{:S(2)}) copy-start(bf16[1024,1024]{1,0:T(8,128)(2,1)} %feat_ref.1) | copy-start | bytes 6291460
  3.6 0.7 copy-start.1

commit v3 on v2

--- a/solution.py
+++ b/solution.py
@@ -47,6 +47,7 @@
     unit, placed, land, fpad, thi, tlo, deg, vpad, grown, gsend, grecv,
     begun, linked, swapped,
     a2a_send, a2a_recv, halo_send, halo_recv, gram_send, gram_recv, swap_send, swap_recv,
+    row_send, row_recv,
 ):
     row, col = lax.axis_index("row"), lax.axis_index("col")
     peers = rows_n * cols_n
@@ -115,6 +116,17 @@
             def _():
                 halo_copy(buf, stage, way, True).wait_send()
 
+    def row_copy(way, x, sending):
+        dr = STEPS[way][0]
+        return pltpu.make_async_remote_copy(
+            src_ref=fpad.at[1 if dr < 0 else th, 1 + x],
+            dst_ref=fpad.at[th + 1 if dr < 0 else 0, 1 + x],
+            send_sem=row_send.at[way, x],
+            recv_sem=row_recv.at[way, x],
+            device_id={"row": snake(trow + dr if sending else trow - dr, rows_n)},
+            device_id_type=pl.DeviceIdType.MESH,
+        )
+
     def corner_copy(way):
         dr, dc = STEPS[way]
         edge = pl.ds(th + 1 if dr < 0 else 0, 1)
@@ -127,10 +139,10 @@
             device_id_type=pl.DeviceIdType.MESH,
         )
 
-    def corner_when(way, action):
+    def corner_when(way, action, ready=True):
         dr, dc = STEPS[way]
 
-        @pl.when(exists(-dr, dc))
+        @pl.when(exists(-dr, dc) & ready)
         def _():
             action(corner_copy(way))
 
@@ -238,30 +250,38 @@
 
     group = max(1, 16 // sw)
     span = group * sw
-    in_block = bw // span
-
-    @pl.loop(0, rows_n // group)
+    strips = bw // sw
+
+    def block_at(step):
+        return lax.rem(row // strips + step, nb)
+
+    @pl.loop(0, nb)
     def _(step):
-        first = lax.rem(row // group + step, rows_n // group)
-        for i in range(group):
-            source = first * group + i
-
-            @pl.when(source != row)
-            def _():
-                strip_copy(0, 0, trow, source).wait_recv()
-
-        rows = pl.ds(pl.multiple_of(lax.rem(first, in_block) * span, span), span)
-        x = 1 + first // in_block
-        if group == 1:
-            for y in range(th):
-                fpad[1 + y, x, rows, :] = land[first, y * sw : (y + 1) * sw, :]
-        else:
-            wide = [land[first * group + i].astype(F32) for i in range(group)]
-            for y in range(th):
-                joined = jnp.concatenate([w[y * sw : (y + 1) * sw] for w in wide], axis=0)
-                fpad[1 + y, x, rows, :] = joined.astype(BF16)
-
-    halo_start(fpad, ITERS, range(4))
+        x = block_at(step)
+        for i in range(strips // group):
+            first = x * strips + i * group
+            for j in range(group):
+                source = first + j
+
+                @pl.when(source != row)
+                def _():
+                    strip_copy(0, 0, trow, source).wait_recv()
+
+            rows = slice(i * span, (i + 1) * span)
+            if group == 1:
+                for y in range(th):
+                    fpad[1 + y, 1 + x, rows, :] = land[first, y * sw : (y + 1) * sw, :]
+            else:
+                wide = [land[first + j].astype(F32) for j in range(group)]
+                for y in range(th):
+                    joined = jnp.concatenate([w[y * sw : (y + 1) * sw] for w in wide], axis=0)
+                    fpad[1 + y, 1 + x, rows, :] = joined.astype(BF16)
+        for way in (0, 1):
+            @pl.when(exists(STEPS[way][0], 0))
+            def _():
+                row_copy(way, x, True).start()
+
+    halo_start(fpad, ITERS, (2, 3))
 
     def tile(y, x, dy, dx):
         offset = (dy + 1) * 3 + dx + 1
@@ -304,11 +324,28 @@
     for y, dy in inner:
         side_tiles(y, dy)
     edges = (((0, -1), 1, (6, 7)), ((th - 1, 1), 0, (4, 5)))
-    for edge, way, corners in edges:
-        halo_wait(fpad, ITERS, (way,))
-        for corner in corners:
-            corner_when(corner, lambda copy: copy.start())
-        tiles(*edge)
+
+    @pl.loop(0, nb)
+    def _(step):
+        x = block_at(step)
+        for (y, dy), way, corners in edges:
+            @pl.when(exists(-STEPS[way][0], 0))
+            def _():
+                row_copy(way, x, False).wait_recv()
+
+            for corner in corners:
+                last = 0 if STEPS[corner][1] < 0 else nb - 1
+                corner_when(corner, lambda copy: copy.start(), x == last)
+            tile(y, x, dy, 0)
+
+            @pl.when(x > 0)
+            def _():
+                tile(y, x - 1, dy, 1)
+
+            @pl.when(x < nb - 1)
+            def _():
+                tile(y, x + 1, dy, -1)
+
     for edge, way, corners in edges:
         halo_wait(fpad, ITERS, corners)
         side_tiles(*edge)
@@ -421,7 +458,15 @@
         def _(other):
             gram_copy(step, lax.rem(me + other, peers), me).wait_send()
 
-    halo_finish(fpad, ITERS, range(4))
+    halo_finish(fpad, ITERS, (2, 3))
+
+    @pl.loop(0, nb)
+    def _(x):
+        for way in (0, 1):
+            @pl.when(exists(STEPS[way][0], 0))
+            def _():
+                row_copy(way, x, True).wait_send()
+
     for way in range(4, 8):
         corner_when(way, lambda copy: copy.wait_send())
 
@@ -476,6 +521,8 @@
             dma((ITERS, peers)),
             dma((3,)),
             dma((3,)),
+            dma((2, nb)),
+            dma((2, nb)),
         ],
         compiler_params=pltpu.CompilerParams(
             collective_id=0, has_side_effects=True, vmem_limit_bytes=48 * 2**20

time: 117 us -> 117 us (level)
  no operation moved by 1% of the time
where the time goes in v3:
time: 117 us
  Pallas kernels  112 us (96%)
  local copies, waits for them, and re-layouts  4.31 us (4%)
    pallas_call x1, Pallas kernels, body(): pl.pallas_call(functools.partial(kernel, rows_n, cols_n, th, nb, sw, scal...  112 us
    unnamed x5, local copies, waits for them, and re-layouts  3.21 us

profile of v3, /device:TPU:0, one launch (start us, length us, event | category | flops | bytes accessed | tf_op | source)
XLA Modules:
  0.0 117.0 jit_solution(6238330401944965655)
XLA Ops:
  0.0 0.7 compare_convert_fusion
  0.7 0.1 copy.6
  0.8 0.1 reshape.13
  0.9 0.1 broadcast_in_dim.11.link_ref
  1.0 0.9 copy.7
  2.0 0.0 copy-start
  2.0 1.6 %copy-done = bf16[1024,1024]{1,0:T(8,128)(2,1)S(1)} copy-done((bf16[1024,1024]{1,0:T(8,128)(2,1)S(1)}, bf16[1024,1024]{1,0:T(8,128)(2,1)}, u32[]{:S(2)}) %copy-start) | copy-done | bytes 2097176
  3.6 0.0 copy-start.1
  3.6 0.7 copy-done.1
  4.3 111.9 %shard_map.46 = f32[32,1024]{1,0:T(8,128)S(1)} custom-call(bf16[1024,1024]{1,0:T(8,128)(2,1)S(1)} %copy-done, s32[1,1024]{1,0:T(1,128)S(1)} %copy-done.1, f32[72,1,128]{2,1,0:T(1,128)S(1)} %broadcast_in_dim.11.link_ref, f32[32,1024]{1,0:T(8,128)S(1)} %bitcast.2), custom_call_target="tpu_custom_call" | custom-call | tf_op jit(solution)/shard_map/pallas_call | solution.py:496
  116.2 0.8 reshape.12
Async XLA Ops:
  2.0 1.6 %copy-start = (bf16[1024,1024]{1,0:T(8,128)(2,1)S(1)}, bf16[1024,1024]{1,0:T(8,128)(2,1)}, u32[]{:S(2)}) copy-start(bf16[1024,1024]{1,0:T(8,128)(2,1)} %feat_ref.1) | copy-start | bytes 6291460
  3.6 0.7 copy-start.1

commit v4 on v2

--- a/solution.py
+++ b/solution.py
@@ -47,6 +47,7 @@
     unit, placed, land, fpad, thi, tlo, deg, vpad, grown, gsend, grecv,
     begun, linked, swapped,
     a2a_send, a2a_recv, halo_send, halo_recv, gram_send, gram_recv, swap_send, swap_recv,
+    solved,
 ):
     row, col = lax.axis_index("row"), lax.axis_index("col")
     peers = rows_n * cols_n
@@ -329,12 +330,23 @@
     inverse = None
     for step in range(ITERS):
         halo_wait(vpad.at[step], step)
+        if step > 1:
+            before = inverse
+
+            @pl.loop(0, (th + 2) * (nb + 2))
+            def _(block):
+                y, x = block // (nb + 2), lax.rem(block, nb + 2)
+                solved[y, x] = jnp.dot(
+                    before, vpad[step, y, x], precision=HIGHEST, preferred_element_type=F32
+                )
+
+        source_of = solved if step > 1 else vpad.at[step]
 
         @pl.loop(0, blocks)
         def _(block):
             y, x = block // nb, lax.rem(block, nb)
             field = jnp.concatenate(
-                [vpad[step, y + o // 3, x + o % 3] for o in range(9)], axis=1
+                [source_of[y + o // 3, x + o % 3] for o in range(9)], axis=1
             )
             high = field.astype(BF16)
             low = (field - high.astype(F32)).astype(BF16)
@@ -346,6 +358,12 @@
             grown[:, pl.ds(pl.multiple_of(block * bw, bw), bw)] = total * deg[block]
 
         value = grown[...]
+        if step + 1 < ITERS:
+            for y in range(th):
+                for x in range(nb):
+                    lo = (y * nb + x) * bw
+                    vpad[step + 1, 1 + y, 1 + x] = value[:, lo : lo + bw]
+            halo_start(vpad.at[step + 1], step + 1)
         if step:
             total = jnp.zeros((part_rows, LANES), F32)
             last = step - 1
@@ -364,12 +382,6 @@
             inverse = whiten(gram)
             value = jnp.dot(inverse, value, precision=HIGHEST, preferred_element_type=F32)
             grown[...] = value
-        if step + 1 < ITERS:
-            for y in range(th):
-                for x in range(nb):
-                    lo = (y * nb + x) * bw
-                    vpad[step + 1, 1 + y, 1 + x] = value[:, lo : lo + bw]
-            halo_start(vpad.at[step + 1], step + 1)
         gram = lax.dot_general(
             value, value, (((1,), (1,)), ((), ())),
             precision=HIGHEST, preferred_element_type=F32,
@@ -476,6 +488,7 @@
             dma((ITERS, peers)),
             dma((3,)),
             dma((3,)),
+            pltpu.VMEM((th + 2, nb + 2, vec_n, bw), F32),
         ],
         compiler_params=pltpu.CompilerParams(
             collective_id=0, has_side_effects=True, vmem_limit_bytes=48 * 2**20

time: 117 us -> 117 us (level)
  no operation moved by 1% of the time
where the time goes in v4:
time: 117 us
  Pallas kernels  112 us (96%)
  local copies, waits for them, and re-layouts  4.31 us (4%)
    pallas_call x1, Pallas kernels, body(): pl.pallas_call(functools.partial(kernel, rows_n, cols_n, th, nb, sw, scal...  112 us
    unnamed x5, local copies, waits for them, and re-layouts  3.21 us

profile of v4, /device:TPU:0, one launch (start us, length us, event | category | flops | bytes accessed | tf_op | source)
XLA Modules:
  0.0 116.8 jit_solution(7829063352587770832)
XLA Ops:
  0.0 0.7 compare_convert_fusion
  0.7 0.1 copy.6
  0.8 0.1 reshape.13
  0.9 0.1 broadcast_in_dim.11.link_ref
  1.0 0.9 copy.7
  2.0 0.0 copy-start
  2.0 1.6 %copy-done = bf16[1024,1024]{1,0:T(8,128)(2,1)S(1)} copy-done((bf16[1024,1024]{1,0:T(8,128)(2,1)S(1)}, bf16[1024,1024]{1,0:T(8,128)(2,1)}, u32[]{:S(2)}) %copy-start) | copy-done | bytes 2097176
  3.6 0.0 copy-start.1
  3.6 0.7 copy-done.1
  4.3 111.7 %shard_map.46 = f32[32,1024]{1,0:T(8,128)S(1)} custom-call(bf16[1024,1024]{1,0:T(8,128)(2,1)S(1)} %copy-done, s32[1,1024]{1,0:T(1,128)S(1)} %copy-done.1, f32[72,1,128]{2,1,0:T(1,128)S(1)} %broadcast_in_dim.11.link_ref, f32[32,1024]{1,0:T(8,128)S(1)} %bitcast.2), custom_call_target="tpu_custom_call" | custom-call | tf_op jit(solution)/shard_map/pallas_call | solution.py:463
  116.0 0.8 reshape.12
Async XLA Ops:
  2.0 1.6 %copy-start = (bf16[1024,1024]{1,0:T(8,128)(2,1)S(1)}, bf16[1024,1024]{1,0:T(8,128)(2,1)}, u32[]{:S(2)}) copy-start(bf16[1024,1024]{1,0:T(8,128)(2,1)} %feat_ref.1) | copy-start | bytes 6291460
  3.6 0.7 copy-start.1

commit v5 on v4

--- a/solution.py
+++ b/solution.py
@@ -203,7 +203,7 @@
 
     @pl.loop(0, supers)
     def _(step):
-        index = lax.rem(trow // per + 1 + step, supers)
+        index = lax.rem(trow // per + supers // 2 + step, supers)
         order = seq_ref[:, pl.ds(pl.multiple_of(index * LANES, LANES), LANES)]
         order = jnp.broadcast_to(order.astype(F32), (LANES, LANES)).T
         lane = lax.broadcasted_iota(jnp.int32, (LANES, LANES), 1).astype(F32)

time: 117 us -> 117 us (level)
  no operation moved by 1% of the time
where the time goes in v5:
time: 117 us
  Pallas kernels  112 us (96%)
  local copies, waits for them, and re-layouts  4.31 us (4%)
    pallas_call x1, Pallas kernels, body(): pl.pallas_call(functools.partial(kernel, rows_n, cols_n, th, nb, sw, scal...  112 us
    unnamed x5, local copies, waits for them, and re-layouts  3.21 us

profile of v5, /device:TPU:0, one launch (start us, length us, event | category | flops | bytes accessed | tf_op | source)
XLA Modules:
  0.0 116.6 jit_solution(10442008105719777978)
XLA Ops:
  0.0 0.7 compare_convert_fusion
  0.7 0.1 copy.6
  0.8 0.1 reshape.13
  0.9 0.1 broadcast_in_dim.11.link_ref
  1.0 0.9 copy.7
  2.0 0.0 copy-start
  2.0 1.6 %copy-done = bf16[1024,1024]{1,0:T(8,128)(2,1)S(1)} copy-done((bf16[1024,1024]{1,0:T(8,128)(2,1)S(1)}, bf16[1024,1024]{1,0:T(8,128)(2,1)}, u32[]{:S(2)}) %copy-start) | copy-done | bytes 2097176
  3.6 0.0 copy-start.1
  3.6 0.7 copy-done.1
  4.3 111.5 %shard_map.46 = f32[32,1024]{1,0:T(8,128)S(1)} custom-call(bf16[1024,1024]{1,0:T(8,128)(2,1)S(1)} %copy-done, s32[1,1024]{1,0:T(1,128)S(1)} %copy-done.1, f32[72,1,128]{2,1,0:T(1,128)S(1)} %broadcast_in_dim.11.link_ref, f32[32,1024]{1,0:T(8,128)S(1)} %bitcast.2), custom_call_target="tpu_custom_call" | custom-call | tf_op jit(solution)/shard_map/pallas_call | solution.py:463
  115.8 0.8 reshape.12
Async XLA Ops:
  2.0 1.6 %copy-start = (bf16[1024,1024]{1,0:T(8,128)(2,1)S(1)}, bf16[1024,1024]{1,0:T(8,128)(2,1)}, u32[]{:S(2)}) copy-start(bf16[1024,1024]{1,0:T(8,128)(2,1)} %feat_ref.1) | copy-start | bytes 6291460
  3.6 0.7 copy-start.1
